TPU v7x, 256 devices: a whole 4x4x8 slice. The times are simulated.
256 devices in a mesh: dp: 16 (over x, y), expert: 16 (over z, core).
Axes of the slice: x: 4, y: 4, z: 8, core: 2. Of those that a mesh axis runs over, the one named last changes fastest.
Arguments:
- tokens: bfloat16 [32768, 1024], P(('dp', 'expert')), may hold values from -6 to 6
- out_grad: bfloat16 [32768, 1024], P(('dp', 'expert')), may hold values from -6 to 6
- expert_ids: int32 [32768, 8], P(('dp', 'expert')), may hold values from 0 to 63, all different within a row; in each aligned block of 128 rows (0 to 127, 128 to 255, ...) at most 24 rows name the same one
- gates: float32 [32768, 8], P(('dp', 'expert')), may hold values from 0.05 to 0.5
- w_gate_up: bfloat16 [64, 1024, 768], P('expert'), may hold values from -0.1875 to 0.1875
- w_down: bfloat16 [64, 384, 1024], P('expert'), may hold values from -0.3125 to 0.3125
Outputs:
- in_grad: bfloat16 [32768, 1024], P(('dp', 'expert'))
- grad_gate_up: float32 [1024, 64, 768], P('dp', 'expert')
- grad_down: float32 [384, 64, 1024], P('dp', 'expert')
Inputs may be any that keep to these rules, and one draw needn't show every extreme that they name: `expert_ids`: among the rows of one device no expert is named more than 24 times, and this bound is reached; each row names 8 different experts.
All inputs are finite; a program needn't handle non-finite values.
Results may differ from a plain program's by a relative error of at most 0.015.
Values may be sent and summed in bfloat16 or wider, within the bound.
No kernel may reach another device: no remote copies, remote signals or barrier semaphores. Data moves between devices by JAX's collectives and lax.ppermute only.
A program may use at most 128 MiB of HBM per device.

v0:
```python
import jax
import jax.numpy as jnp
from jax import lax
from jax.sharding import PartitionSpec as P


def recompute(x_recv, w_gate_up, hidden_units):
    both = jnp.einsum("sjcd,jdf->sjcf", x_recv, w_gate_up, preferred_element_type=jnp.float32)
    gate_pre = both[..., :hidden_units]
    up_val = both[..., hidden_units:]
    sig = jax.nn.sigmoid(gate_pre)
    act = gate_pre * sig
    hidden = (act * up_val).astype(jnp.bfloat16)
    return (gate_pre, up_val, sig, act, hidden)


def per_device(tokens, out_grad, expert_ids, gates, w_gate_up, w_down):
    n_owner = lax.axis_size("expert")
    tok_dev, top = expert_ids.shape
    exp_dev, width, double = w_gate_up.shape
    hidden_units = double // 2
    experts = exp_dev * n_owner
    slots = max(2, 3 * tok_dev * top // (2 * experts))
    flat_ids = expert_ids.reshape(-1)
    onehot = (flat_ids[:, None] == jnp.arange(experts, dtype=jnp.int32)[None, :]).astype(jnp.int32)
    earlier = jnp.cumsum(onehot, axis=0) - onehot
    slot = jnp.sum(earlier * onehot, axis=1)
    target = flat_ids * slots + slot
    token_rows = jnp.repeat(tokens, top, axis=0)
    scaled_rows = (
        gates.reshape(-1, 1) * jnp.repeat(out_grad, top, axis=0).astype(jnp.float32)
    ).astype(jnp.bfloat16)
    layout = (n_owner, exp_dev, slots, width)
    x_send = (
        jnp.zeros((experts * slots, width), jnp.bfloat16).at[target].set(token_rows).reshape(layout)
    )
    s_send = (
        jnp.zeros((experts * slots, width), jnp.bfloat16)
        .at[target]
        .set(scaled_rows)
        .reshape(layout)
    )
    x_recv, s_recv = (
        lax.all_to_all(x_send, "expert", split_axis=0, concat_axis=0, tiled=True),
        lax.all_to_all(s_send, "expert", split_axis=0, concat_axis=0, tiled=True),
    )
    gate_pre, up_val, sig, act, hidden = recompute(x_recv, w_gate_up, hidden_units)
    dh = jnp.einsum("sjcd,jfd->sjcf", s_recv, w_down, preferred_element_type=jnp.float32)
    d_gate = dh * up_val * sig * (1.0 + gate_pre * (1.0 - sig))
    d_up = dh * act
    d_both = jnp.concatenate([d_gate, d_up], axis=-1).astype(jnp.bfloat16)
    grad_gu = lax.psum_scatter(
        jnp.einsum("sjcd,sjcf->djf", x_recv, d_both, preferred_element_type=jnp.float32).astype(
            jnp.bfloat16
        ),
        "dp",
        scatter_dimension=0,
        tiled=True,
    ).astype(jnp.float32)
    grad_dn = lax.psum_scatter(
        jnp.einsum("sjcf,sjcd->fjd", hidden, s_recv, preferred_element_type=jnp.float32).astype(
            jnp.bfloat16
        ),
        "dp",
        scatter_dimension=0,
        tiled=True,
    ).astype(jnp.float32)
    grad_gu, grad_dn = (grad_gu, grad_dn)
    route_grad = jnp.einsum(
        "sjcf,jdf->sjcd", d_both, w_gate_up, preferred_element_type=jnp.float32
    ).astype(jnp.bfloat16)
    returned = lax.all_to_all(
        route_grad, "expert", split_axis=0, concat_axis=0, tiled=True
    ).reshape(experts * slots, width)
    picked = returned[target].astype(jnp.float32).reshape(tok_dev, top, width)
    in_grad = jnp.sum(picked, axis=1).astype(jnp.bfloat16)
    return (in_grad, grad_gu, grad_dn)


def solution(mesh):
    in_specs = (
        P(("dp", "expert"), None),
        P(("dp", "expert"), None),
        P(("dp", "expert"), None),
        P(("dp", "expert"), None),
        P("expert", None, None),
        P("expert", None, None),
    )
    out_specs = (P(("dp", "expert"), None), P("dp", "expert", None), P("dp", "expert", None))
    return jax.shard_map(
        per_device, mesh=mesh, in_specs=in_specs, out_specs=out_specs, check_vma=False
    )
```

profile of v0, /device:TPU:1, one launch (start us, length us, event | category | flops | bytes accessed | tf_op | source)
XLA Modules:
  0.0 414.2 jit_solution(136329357481510448)
XLA Ops:
  7.2 0.0 copy-start
  7.2 0.8 broadcast_multiply_fusion
  8.0 0.9 copy.23
  8.9 0.1 eq.29
  9.0 0.1 eq.25
  9.1 0.1 copy.22
  9.2 0.1 mul.52
  9.3 0.7 fusion.37
  10.0 31.1 %reduce-window.6 = s32[64,8,128]{2,1,0:T(8,128)S(1)} reduce-window(s32[64,8,128]{2,1,0:T(8,128)} %fusion.37, s32[]{:T(128)} %constant.7.clone.1), window={size=1x1x128 pad=0_0x0_0x127_0}, to_apply=%region_0.0 | reduce-window | flops 8323072 | bytes 524292 | tf_op jit(solution)/shard_map/reduce-window
  41.1 0.8 slice.18
  42.0 1.1 copy.25
  43.1 0.1 copy.26
  43.2 0.1 broadcast_add_fusion
  43.3 0.1 fusion.36
  43.4 7.7 %scatter_custom_fusion.1 = bf16[1536,1024]{1,0:T(8,128)(2,1)} fusion(s32[1024]{0:T(1024)S(1)} %bitcast.86, bf16[]{:T(256)} %constant.5.clone.1, bf16[128,1024]{1,0:T(8,128)(2,1)} %param.6), kind=kCustom, calls=%fused_computation.32 | custom fusion | bytes 3407874 | tf_op jit(solution)/shard_map/scatter | solution.py:35
  51.1 0.0 copy-start.2
  51.2 0.0 copy-start.3
  51.2 10.1 %all-to-all-start.1 = ((bf16[16,4,24,1024]{3,2,1,0:T(8,128)(2,1)}), bf16[16,4,24,1024]{3,2,1,0:T(8,128)(2,1)}, u32[]{:S(2)}, u32[]{:S(2)}) async-start(bf16[16,4,24,1024]{3,2,1,0:T(8,128)(2,1)} %bitcast.82), calls=%async_computation.1 | async-start | bytes 6291456 | tf_op jit(solution)/shard_map/all_to_all | solution.py:44
  61.3 0.0 copy-done.2
  61.3 0.8 convert_element_type.50
  62.1 0.0 copy-done.3
  62.1 0.1 copy.27
  62.2 0.1 mul.54
  62.3 8.1 %scatter_custom_fusion = bf16[1536,1024]{1,0:T(8,128)(2,1)} fusion(s32[1024]{0:T(1024)S(1)} %bitcast.87, f32[128,1024]{1,0:T(8,128)} %convert_element_type.50, f32[1024]{0:T(1024)S(1)} %mul.54, bf16[]{:T(256)} %constant.5.clone.1), kind=kCustom, calls=%fused_computation.30 | custom fusion | flops 2097152 | bytes 3674114 | tf_op jit(solution)/shard_map/scatter | solution.py:40
  70.4 62.0 %all-to-all-done.1 = bf16[16,4,24,1024]{3,2,1,0:T(8,128)(2,1)} async-done(((bf16[16,4,24,1024]{3,2,1,0:T(8,128)(2,1)}), bf16[16,4,24,1024]{3,2,1,0:T(8,128)(2,1)}, u32[]{:S(2)}, u32[]{:S(2)}) %all-to-all-start.1) | async-done | bytes 3145760 | tf_op jit(solution)/shard_map/all_to_all | solution.py:44
  132.4 5.4 %all-to-all-start = ((bf16[16,4,24,1024]{3,2,1,0:T(8,128)(2,1)}), bf16[16,4,24,1024]{3,2,1,0:T(8,128)(2,1)}, u32[]{:S(2)}, u32[]{:S(2)}) async-start(bf16[16,4,24,1024]{3,2,1,0:T(8,128)(2,1)} %bitcast.81), calls=%async_computation | async-start | bytes 6291456 | tf_op jit(solution)/shard_map/all_to_all | solution.py:45
  137.8 0.2 all-reduce.5.cloned.1.call-start
  138.0 8.5 %fusion.17 = f32[16,4,24,768]{3,2,0,1:T(8,128)} fusion(bf16[4,1024,768]{2,1,0:T(8,128)(2,1)} %param.10, bf16[16,4,24,1024]{3,2,1,0:T(8,128)(2,1)} %all-to-all-done.1), kind=kOutput, calls=%fused_computation.29 | convolution fusion | flops 2415919104 | bytes 14155776 | tf_op jit(solution)/shard_map/sjcd,jdf->sjcf/dot_general | solution.py:8
  146.5 62.4 %all-to-all-done = bf16[16,4,24,1024]{3,2,1,0:T(8,128)(2,1)} async-done(((bf16[16,4,24,1024]{3,2,1,0:T(8,128)(2,1)}), bf16[16,4,24,1024]{3,2,1,0:T(8,128)(2,1)}, u32[]{:S(2)}, u32[]{:S(2)}) %all-to-all-start) | async-done | bytes 3145760 | tf_op jit(solution)/shard_map/all_to_all | solution.py:45
  208.9 0.0 copy-done
  208.9 6.8 %fusion.14 = (bf16[16,4,24,384]{3,2,0,1:T(8,128)(2,1)S(1)}, bf16[16,4,24,384]{3,2,0,1:T(8,128)(2,1)S(1)}, bf16[16,4,24,384]{3,2,0,1:T(8,128)(2,1)}) fusion(f32[16,4,24,768]{3,2,0,1:T(8,128)} %fusion.17, bf16[4,384,1024]{2,1,0:T(8,128)(2,1)S(1)} %copy-done, bf16[16,4,24,1024]{3,2,1,0:T(8,128)(2,1)} %all-to-all-done), kind=kOutput, calls=%fused_computation.24 | convolution fusion | flops 1216806912 | bytes 14548992 | tf_op jit(solution)/shard_map/sjcd,jfd->sjcf/dot_general | solution.py:48
  215.7 0.0 copy-start.5
  215.7 0.0 copy-start.6
  215.7 1.1 copy-done.5
  216.7 0.4 copy-done.6
  217.1 7.4 %fusion = bf16[1024,4,768]{0,2,1:T(8,128)(2,1)} fusion(bf16[16,4,24,1024]{3,2,1,0:T(8,128)(2,1)} %all-to-all-done.1, bf16[16,4,24,384]{3,2,0,1:T(8,128)(2,1)S(1)} %get-tuple-element.12, bf16[16,4,24,384]{3,2,0,1:T(8,128)(2,1)S(1)} %get-tuple-element.11), kind=kOutput, calls=%fused_computation.4 | convolution fusion | flops 2423783424 | bytes 11796480 | tf_op jit(solution)/shard_map/sjcd,sjcf->djf/dot_general | solution.py:53
  224.4 10.8 %copy.32 = bf16[1024,4,768]{2,1,0:T(4,128)(2,1)} copy(bf16[1024,4,768]{0,2,1:T(8,128)(2,1)} %fusion) | data formatting | bytes 12582912 | tf_op jit(solution)/shard_map/convert_element_type | solution.py:53
  235.2 4.3 %fusion.6 = bf16[384,4,1024]{0,2,1:T(8,128)(2,1)S(1)} fusion(bf16[16,4,24,1024]{3,2,1,0:T(8,128)(2,1)} %all-to-all-done, bf16[16,4,24,384]{3,2,0,1:T(8,128)(2,1)} %get-tuple-element.13), kind=kOutput, calls=%fused_computation.12 | convolution fusion | flops 1209532416 | bytes 7471104 | tf_op jit(solution)/shard_map/sjcf,sjcd->fjd/dot_general | solution.py:61
  239.5 4.5 %copy.34 = bf16[384,4,1024]{2,1,0:T(4,128)(2,1)} copy(bf16[384,4,1024]{0,2,1:T(8,128)(2,1)S(1)} %fusion.6) | data formatting | bytes 6291456 | tf_op jit(solution)/shard_map/convert_element_type | solution.py:61
  244.0 0.0 all-reduce.5.cloned.1.call-update
  244.0 6.2 %convert_bitcast_fusion = bf16[16,4,24,1024]{3,2,0,1:T(8,128)(2,1)S(1)} fusion(bf16[4,1024,768]{2,1,0:T(8,128)(2,1)} %param.10, bf16[16,4,24,384]{3,2,0,1:T(8,128)(2,1)} %copy-done.6, bf16[16,4,24,384]{3,2,0,1:T(8,128)(2,1)} %copy-done.5), kind=kOutput, calls=%fused_computation.16 | convolution fusion | flops 2422210560 | bytes 11796480 | tf_op jit(solution)/shard_map/sjcf,jdf->sjcd/dot_general | solution.py:69
  250.2 2.1 copy.30
  252.3 0.0 copy-start.4
  252.3 5.6 %all-to-all-start.2 = ((bf16[16,4,24,1024]{3,2,1,0:T(8,128)(2,1)}), bf16[16,4,24,1024]{3,2,1,0:T(8,128)(2,1)}, u32[]{:S(2)}, u32[]{:S(2)}) async-start(bf16[16,4,24,1024]{3,2,1,0:T(8,128)(2,1)} %copy.30), calls=%async_computation.2 | async-start | bytes 6291456 | tf_op jit(solution)/shard_map/all_to_all | solution.py:72
  257.9 0.0 copy-done.4
  257.9 0.6 dynamic-slice
  259.8 69.2 %all-to-all-done.2 = bf16[16,4,24,1024]{3,2,1,0:T(8,128)(2,1)} async-done(((bf16[16,4,24,1024]{3,2,1,0:T(8,128)(2,1)}), bf16[16,4,24,1024]{3,2,1,0:T(8,128)(2,1)}, u32[]{:S(2)}, u32[]{:S(2)}) %all-to-all-start.2) | async-done | bytes 3145760 | tf_op jit(solution)/shard_map/all_to_all | solution.py:72
  329.0 0.0 copy-start.1
  329.0 8.5 %gather_fusion = bf16[1024,1024]{1,0:T(8,128)(2,1)} fusion(bf16[1536,1024]{1,0:T(8,128)(2,1)} %bitcast.15, s32[1024]{0:T(1024)S(1)} %broadcast_clamp_fusion), kind=kCustom, calls=%fused_computation | custom fusion | bytes 4198400 | tf_op jit(solution)/shard_map/gather | solution.py:75
  337.5 3.7 bitcast_reduce_fusion
  341.2 62.5 %all-reduce.5.cloned.1.call-done = (bf16[1024,4,768]{2,1,0:T(4,128)(2,1)}, bf16[384,4,1024]{2,1,0:T(4,128)(2,1)}) async-done(((bf16[1024,4,768]{2,1,0:T(4,128)(2,1)}, bf16[384,4,1024]{2,1,0:T(4,128)(2,1)}), (bf16[1024,4,768]{2,1,0:T(4,128)(2,1)}, bf16[384,4,1024]{2,1,0:T(4,128)(2,1)})) %all-reduce.5.cloned.1.call-update) | async-done | bytes 9437200
  403.7 1.9 dynamic-slice_convert_fusion
  405.6 1.7 dynamic-slice_convert_fusion.1
  407.3 0.0 copy-done.1
  (4 shorter events, 0.0 us)
Async XLA Ops:
  7.2 201.7 %copy-start = (bf16[4,384,1024]{2,1,0:T(8,128)(2,1)S(1)}, bf16[4,384,1024]{2,1,0:T(8,128)(2,1)}, u32[]{:S(2)}) copy-start(bf16[4,384,1024]{2,1,0:T(8,128)(2,1)} %param.11) | copy-start | bytes 9437188
  51.1 10.1 %copy-start.2 = (bf16[128,1024]{1,0:T(8,128)(2,1)S(1)}, bf16[128,1024]{1,0:T(8,128)(2,1)}, u32[]{:S(2)}) copy-start(bf16[128,1024]{1,0:T(8,128)(2,1)} %param.7) | copy-start | bytes 786436
  51.2 11.0 %copy-start.3 = (f32[128,8]{0,1:T(8,128)S(1)}, f32[128,8]{0,1:T(8,128)}, u32[]{:S(2)}) copy-start(f32[128,8]{0,1:T(8,128)} %param.9) | copy-start | bytes 12292
  51.2 81.2 %all-to-all-start.1 = ((bf16[16,4,24,1024]{3,2,1,0:T(8,128)(2,1)}), bf16[16,4,24,1024]{3,2,1,0:T(8,128)(2,1)}, u32[]{:S(2)}, u32[]{:S(2)}) async-start(bf16[16,4,24,1024]{3,2,1,0:T(8,128)(2,1)} %bitcast.82), calls=%async_computation.1 | async-start | bytes 6291456 | tf_op jit(solution)/shard_map/all_to_all | solution.py:44
  132.4 76.5 %all-to-all-start = ((bf16[16,4,24,1024]{3,2,1,0:T(8,128)(2,1)}), bf16[16,4,24,1024]{3,2,1,0:T(8,128)(2,1)}, u32[]{:S(2)}, u32[]{:S(2)}) async-start(bf16[16,4,24,1024]{3,2,1,0:T(8,128)(2,1)} %bitcast.81), calls=%async_computation | async-start | bytes 6291456 | tf_op jit(solution)/shard_map/all_to_all | solution.py:45
  137.8 265.9 %all-reduce.5.cloned.1.call-start = ((), (), s32[]{:S(2)}) async-start(), calls=%async_computation.3 | async-start | bytes 18874368
  215.7 1.1 copy-start.5
  215.7 1.4 copy-start.6
  252.3 5.6 %copy-start.4 = (u32[256]{0:T(256)S(1)}, u32[256]{0:T(256)}, u32[]{:S(2)}) copy-start(u32[256]{0:T(256)} %constant.25) | copy-start | bytes 3076
  252.3 76.7 %all-to-all-start.2 = ((bf16[16,4,24,1024]{3,2,1,0:T(8,128)(2,1)}), bf16[16,4,24,1024]{3,2,1,0:T(8,128)(2,1)}, u32[]{:S(2)}, u32[]{:S(2)}) async-start(bf16[16,4,24,1024]{3,2,1,0:T(8,128)(2,1)} %copy.30), calls=%async_computation.2 | async-start | bytes 6291456 | tf_op jit(solution)/shard_map/all_to_all | solution.py:72
  329.0 78.4 %copy-start.1 = (bf16[4,384,1024]{2,1,0:T(8,128)(2,1)S(1)}, bf16[4,384,1024]{2,1,0:T(8,128)(2,1)}, u32[]{:S(2)}) copy-start(bf16[4,384,1024]{2,1,0:T(8,128)(2,1)} %param.11) | copy-start | bytes 9437188
Sparse Core Ops, SparseCore 0:
  244.1 159.4 all-reduce.4
where the time goes:
time: 416 us; the launch traced here: 414 us
  waiting for transfers between devices  256 us (62%)
  other arithmetic  49.2 us (12%)
  local copies, waits for them, and re-layouts  39.1 us (9%)
  matrix products  33.1 us (8%)
  starting transfers between devices  21.4 us (5%)
  between operations  15.4 us (4%)
    all_to_all x1, waiting for transfers between devices, per_device(): lax.all_to_all(route_grad, 'expert', split_axis=0, concat_axis=0, tiled=T...  69.2 us
    unnamed x2, waiting for transfers between devices  62.5 us
    all_to_all x1, waiting for transfers between devices, per_device(): lax.all_to_all(s_send, 'expert', split_axis=0, concat_axis=0, tiled=True)  62.4 us
    all_to_all x1, waiting for transfers between devices, per_device(): lax.all_to_all(x_send, 'expert', split_axis=0, concat_axis=0, tiled=True)  62 us
    another operation x3, other arithmetic  31.3 us
    convert_element_type x1, local copies, waits for them, and re-layouts, per_device(): jnp.einsum('sjcd,sjcf->djf', x_recv, d_both, preferred_element_type=jnp.f...  10.8 us
    all_to_all x1, starting transfers between devices, per_device(): lax.all_to_all(x_send, 'expert', split_axis=0, concat_axis=0, tiled=True)  10.1 us
    gather x1, local copies, waits for them, and re-layouts, per_device(): picked = returned[target].astype(jnp.float32).reshape(tok_dev, top, width)  8.52 us
  transfers between devices with their start and end apart: 4, of which 4 were waited for; matrix products, arithmetic and copies ran while one was open for 9% of the time, Pallas kernels for 0%

commit v1 on v0

v1 whole, which is shorter than its diff:
```python
import functools

import jax
import jax.numpy as jnp
from jax import lax
from jax.experimental import pallas as pl
from jax.experimental.pallas import tpu as pltpu
from jax.sharding import PartitionSpec as P

TOK = 128
TOP = 8
D = 1024
FF = 384
CAP = 24
EXP = 4
OWN = 16
SIDE = 4
GU_ROWS = D // 16
DN_ROWS = FF // 16
PAIR = 2 * CAP
ROWS = OWN * CAP
BLK = 2 * (3 * GU_ROWS // 4 + DN_ROWS)
CUT = 80
BF = jnp.bfloat16
F32 = jnp.float32
MB = 1 << 20


def dot(a, b, dims):
    return lax.dot_general(a, b, (dims, ((), ())), preferred_element_type=F32)


NN = ((1,), (0,))
NT = ((1,), (1,))
TN = ((0,), (0,))


def vmem(limit):
    return pltpu.CompilerParams(vmem_limit_bytes=limit * MB)


def prep_kernel(x_ref, g_ref, ids_ref, gates_ref, out_ref):
    out_ref[:, :D] = x_ref[...]
    out_ref[:, D : 2 * D] = g_ref[...]
    gate = gates_ref[...]
    high = gate.astype(BF)
    rest = gate - high.astype(F32)
    mid = rest.astype(BF)
    low = (rest - mid.astype(F32)).astype(BF)
    out_ref[:, 2 * D :] = jnp.zeros((TOK, 128), BF)
    top = jnp.concatenate([ids_ref[...].astype(F32).astype(BF), high], axis=0)
    out_ref[0:16, 2 * D :] = top
    out_ref[16:32, 2 * D :] = jnp.concatenate([mid, low], axis=0)


def prep(tokens, out_grad, ids_t, gates_t):
    return pl.pallas_call(
        prep_kernel,
        out_shape=jax.ShapeDtypeStruct((TOK, 2 * D + 128), BF),
        cost_estimate=pl.CostEstimate(flops=0, bytes_accessed=MB, transcendentals=0),
    )(tokens, out_grad, ids_t, gates_t)


def route_kernel(q_ref, pay_ref, x_ref, s_ref, oh_ref):
    first = (q_ref[0] * EXP).astype(F32)
    before = (
        lax.broadcasted_iota(jnp.int32, (TOK, TOK), 0)
        < lax.broadcasted_iota(jnp.int32, (TOK, TOK), 1)
    ).astype(BF)
    named, gate = [], []
    for i in range(2):
        meta_a = pay_ref[i, 0:16, 2 * D :].astype(F32)
        meta_b = pay_ref[i, 16:32, 2 * D :].astype(F32)
        ids = meta_a[0:TOP]
        gates = (meta_a[TOP:] + meta_b[0:TOP]) + meta_b[TOP:]
        for j in range(EXP):
            hit = ids == first + float(j)
            named.append(jnp.sum(jnp.where(hit, 1.0, 0.0), axis=0, keepdims=True))
            gate.append(jnp.sum(jnp.where(hit, gates, 0.0), axis=0, keepdims=True))
    mask = jnp.concatenate(named, axis=0)
    rank = dot(mask.astype(BF), before, NN)
    target = jnp.where(mask > 0.5, rank, -1000.0)
    row = lax.broadcasted_iota(jnp.int32, (PAIR, 2 * TOK), 0).astype(F32)
    picks, weights = [], []
    for j in range(EXP):
        place = jnp.concatenate([target[j : j + 1], target[EXP + j : EXP + j + 1] + float(CAP)], axis=1)
        gates = jnp.concatenate([gate[j], gate[EXP + j]], axis=1)
        hit = row == place
        picks.append(jnp.where(hit, 1.0, 0.0))
        weights.append(jnp.sum(jnp.where(hit, gates, 0.0), axis=1, keepdims=True))
    pick = jnp.concatenate(picks, axis=0).astype(BF)
    weight = jnp.concatenate(weights, axis=0)
    oh_ref[0] = pick
    x = pay_ref[:, :, :D].reshape(2 * TOK, D)
    g = pay_ref[:, :, D : 2 * D].reshape(2 * TOK, D)
    x_rows = dot(pick, x, NN).astype(BF)
    s_rows = (dot(pick, g, NN) * weight).astype(BF)
    for j in range(EXP):
        x_ref[j] = x_rows[j * PAIR : (j + 1) * PAIR]
        s_ref[j] = s_rows[j * PAIR : (j + 1) * PAIR]


def route(q, pay):
    pairs = OWN // 2
    rows = jax.ShapeDtypeStruct((EXP, ROWS, D), BF)
    spec = pl.BlockSpec((EXP, PAIR, D), lambda i, q: (0, i, 0))
    return pl.pallas_call(
        route_kernel,
        out_shape=(rows, rows, jax.ShapeDtypeStruct((pairs, EXP * PAIR, 2 * TOK), BF)),
        grid_spec=pltpu.PrefetchScalarGridSpec(
            num_scalar_prefetch=1,
            grid=(pairs,),
            in_specs=[pl.BlockSpec((2, TOK, 2 * D + 128), lambda i, q: (i, 0, 0))],
            out_specs=(spec, spec, pl.BlockSpec((1, EXP * PAIR, 2 * TOK), lambda i, q: (i, 0, 0))),
        ),
        compiler_params=vmem(32),
        cost_estimate=pl.CostEstimate(flops=2 * 2 * 1536 * 256 * D, bytes_accessed=15 * MB, transcendentals=0),
    )(q, pay)


def grads_kernel(where_ref, x_ref, s_ref, wgu_ref, wdn_ref, o0, o1, o3, o2a, o2b, d_ref, pgu, pdn):
    jj = pl.program_id(0)
    x, s = x_ref[0], s_ref[0]
    both = dot(x, wgu_ref[0], NN)
    gate_pre, up_val = both[:, :FF], both[:, FF:]
    sig = jax.nn.sigmoid(gate_pre)
    act = gate_pre * sig
    hidden = (act * up_val).astype(BF)
    dh = dot(s, wdn_ref[0], NT)
    d_gate = dh * up_val * sig * (1.0 + gate_pre * (1.0 - sig))
    d_both = jnp.concatenate([d_gate, dh * act], axis=1).astype(BF)
    d_ref[0] = d_both
    pgu[...] = dot(x, d_both, TN)
    pdn[jj] = dot(hidden, s, TN)

    def outs():
        for first in range(SIDE):
            for second in range(SIDE):
                if first == 2:
                    ref, at = (o2a, second) if second < 2 else (o2b, second - 2)
                else:
                    ref, at = {0: o0, 1: o1, 3: o3}[first], second
                yield first * SIDE + second, ref, at

    for step in range(2):

        @pl.when(jj == step)
        def _():
            for number, ref, at in outs():
                base = pl.multiple_of(where_ref[number] * GU_ROWS, GU_ROWS)
                for a in range(4):
                    for b in range(3):
                        n = a * 3 + b
                        ref[at, 48 * step + 16 * (n // 4) : 48 * step + 16 * (n // 4) + 16, 256 * (n % 4) : 256 * (n % 4) + 256] = pgu[pl.ds(base + 16 * a, 16), 256 * b : 256 * b + 256].astype(BF)
                if step == 1:
                    low = pl.multiple_of(where_ref[number] * DN_ROWS, DN_ROWS)
                    ref[at, 96:BLK, :] = jnp.concatenate([pdn[0, pl.ds(low, DN_ROWS), :], pdn[1, pl.ds(low, DN_ROWS), :]], axis=0).astype(BF)


def grads(half, where, x_rows, s_rows, w_gate_up, w_down):
    def at(j, w):
        return (2 * half + j, 0, 0)

    def whole(j, w):
        return (0, 0, 0)

    def shape(n):
        return jax.ShapeDtypeStruct((n, BLK, D), BF)

    counts = (4, 4, 4, 2, 2)
    return pl.pallas_call(
        grads_kernel,
        out_shape=tuple(shape(n) for n in counts) + (jax.ShapeDtypeStruct((2, ROWS, 2 * FF), BF),),
        grid_spec=pltpu.PrefetchScalarGridSpec(
            num_scalar_prefetch=1,
            grid=(2,),
            in_specs=[
                pl.BlockSpec((1, ROWS, D), at),
                pl.BlockSpec((1, ROWS, D), at),
                pl.BlockSpec((1, D, 2 * FF), at),
                pl.BlockSpec((1, FF, D), at),
            ],
            out_specs=tuple(pl.BlockSpec((n, BLK, D), whole) for n in counts) + (pl.BlockSpec((1, ROWS, 2 * FF), lambda j, w: (j, 0, 0)),),
            scratch_shapes=[pltpu.VMEM((D, 2 * FF), F32), pltpu.VMEM((2, FF, D), F32)],
        ),
        compiler_params=vmem(48),
        cost_estimate=pl.CostEstimate(flops=2 * 2 * ROWS * D * FF * 6, bytes_accessed=12 * MB, transcendentals=0),
    )(where, x_rows, s_rows, w_gate_up, w_down)


def back_kernel(da_ref, db_ref, wgu_ref, oh_ref, out_ref, rg):
    j = pl.program_id(0)

    @pl.when(j < 2)
    def _():
        rg[j] = dot(da_ref[0], wgu_ref[0], NT).astype(BF)

    @pl.when(j >= 2)
    def _():
        rg[j] = dot(db_ref[0], wgu_ref[0], NT).astype(BF)

    @pl.when(j == EXP - 1)
    def _():
        for i in range(OWN // 2):
            rows = jnp.concatenate([rg[n, i * PAIR : (i + 1) * PAIR, :] for n in range(EXP)], axis=0)
            out_ref[2 * i * TOK : 2 * (i + 1) * TOK, :] = dot(oh_ref[i], rows, TN).astype(BF)


def back(d_a, d_b, w_gate_up, oh):
    return pl.pallas_call(
        back_kernel,
        out_shape=jax.ShapeDtypeStruct((OWN * TOK, D), BF),
        grid=(EXP,),
        in_specs=[
            pl.BlockSpec((1, ROWS, 2 * FF), lambda j: (jnp.minimum(j, 1), 0, 0)),
            pl.BlockSpec((1, ROWS, 2 * FF), lambda j: (jnp.maximum(j - 2, 0), 0, 0)),
            pl.BlockSpec((1, D, 2 * FF), lambda j: (j, 0, 0)),
            pl.BlockSpec((OWN // 2, EXP * PAIR, 2 * TOK), lambda j: (0, 0, 0)),
        ],
        out_specs=pl.BlockSpec((OWN * TOK, D), lambda j: (0, 0)),
        scratch_shapes=[pltpu.VMEM((EXP, ROWS, D), BF)],
        compiler_params=vmem(40),
        cost_estimate=pl.CostEstimate(flops=2 * 1536 * D * (2 * FF + 256), bytes_accessed=16 * MB, transcendentals=0),
    )(d_a, d_b, w_gate_up, oh)


def add1_kernel(o1, ra, o3, rb, s1, s3):
    s1[0:2] = (o1[0:2].astype(F32) + ra[...].astype(F32)).astype(BF)
    s1[2:4] = o1[2:4]
    s3[0:2] = o3[0:2]
    s3[2:4] = (o3[2:4].astype(F32) + rb[...].astype(F32)).astype(BF)


def add1(o1, ra, o3, rb):
    out = jax.ShapeDtypeStruct((SIDE, BLK, D), BF)
    return pl.pallas_call(
        add1_kernel,
        out_shape=(out, out),
        compiler_params=vmem(32),
        cost_estimate=pl.CostEstimate(flops=0, bytes_accessed=6 * MB, transcendentals=0),
    )(o1, ra, o3, rb)


def add2_kernel(o0, r1, r3, f0, f1, f3, f2a, f2b):
    def total(k):
        return (o0[k].astype(F32) + r1[k].astype(F32)) + r3[k].astype(F32)

    f0[...] = total(0)
    f1[...] = total(1).astype(BF)
    f3[...] = total(3).astype(BF)
    two = total(2).astype(BF)
    f2a[...] = two[:CUT]
    f2b[...] = two[CUT:]


def add2(o0, r1, r3):
    whole = jax.ShapeDtypeStruct((BLK, D), BF)
    return pl.pallas_call(
        add2_kernel,
        out_shape=(
            jax.ShapeDtypeStruct((BLK, D), F32),
            whole,
            whole,
            jax.ShapeDtypeStruct((CUT, D), BF),
            jax.ShapeDtypeStruct((BLK - CUT, D), BF),
        ),
        compiler_params=vmem(32),
        cost_estimate=pl.CostEstimate(flops=0, bytes_accessed=5 * MB, transcendentals=0),
    )(o0, r1, r3)


def add3_kernel(f1, ra, f3, rb, s1, s3):
    s1[:CUT] = (f1[:CUT].astype(F32) + ra[...].astype(F32)).astype(BF)
    s1[CUT:] = f1[CUT:]
    s3[:CUT] = f3[:CUT]
    s3[CUT:] = (f3[CUT:].astype(F32) + rb[...].astype(F32)).astype(BF)


def add3(f1, ra, f3, rb):
    out = jax.ShapeDtypeStruct((BLK, D), BF)
    return pl.pallas_call(
        add3_kernel,
        out_shape=(out, out),
        cost_estimate=pl.CostEstimate(flops=0, bytes_accessed=MB, transcendentals=0),
    )(f1, ra, f3, rb)


def last_kernel(a0, a1, a3, b0, b1, b3, gu_ref, dn_ref):
    for half, (f0, r1, r3) in enumerate(((a0, a1, a3), (b0, b1, b3))):
        total = f0[...] + r1[...].astype(F32) + r3[...].astype(F32)
        for e in range(2):
            for a in range(4):
                for b in range(3):
                    n = a * 3 + b
                    gu_ref[16 * a : 16 * a + 16, 2 * FF * (2 * half + e) + 256 * b : 2 * FF * (2 * half + e) + 256 * b + 256] = total[48 * e + 16 * (n // 4) : 48 * e + 16 * (n // 4) + 16, 256 * (n % 4) : 256 * (n % 4) + 256]
            dn_ref[:, D * (2 * half + e) : D * (2 * half + e + 1)] = total[96 + DN_ROWS * e : 96 + DN_ROWS * (e + 1), :]


def last(*pieces):
    return pl.pallas_call(
        last_kernel,
        out_shape=(
            jax.ShapeDtypeStruct((GU_ROWS, EXP * 2 * FF), F32),
            jax.ShapeDtypeStruct((DN_ROWS, EXP * D), F32),
        ),
        compiler_params=vmem(32),
        cost_estimate=pl.CostEstimate(flops=0, bytes_accessed=4 * MB, transcendentals=0),
    )(*pieces)


def along(axis, step):
    pairs = []
    for i in range(SIDE * SIDE):
        x, y = divmod(i, SIDE)
        x, y = ((x + step) % SIDE, y) if axis == 0 else (x, (y + step) % SIDE)
        pairs.append((i, x * SIDE + y))
    return pairs


def move(block, axis, step):
    return lax.ppermute(block, "dp", along(axis, step))


def stage_one(axis, o0, o1, o3, o2a, o2b):
    ra, rb = move(o2a, axis, 1), move(o2b, axis, -1)
    s1, s3 = add1(o1, ra, o3, rb)
    r1, r3 = move(s1, axis, 1), move(s3, axis, -1)
    return add2(o0, r1, r3)


def stage_two(axis, f0, f1, f3, f2a, f2b):
    ra, rb = move(f2a, axis, 1), move(f2b, axis, -1)
    s1, s3 = add3(f1, ra, f3, rb)
    return f0, move(s1, axis, 1), move(s3, axis, -1)


def per_device(tokens, out_grad, expert_ids, gates, w_gate_up, w_down):
    p, q = lax.axis_index("dp"), lax.axis_index("expert")
    px, py = p // SIDE, p % SIDE
    near = jnp.arange(SIDE, dtype=jnp.int32)
    xs, ys = (px + near) % SIDE, (py + near) % SIDE
    where_a = (xs[:, None] * SIDE + ys[None, :]).reshape(-1).astype(jnp.int32)
    where_b = (xs[None, :] * SIDE + ys[:, None]).reshape(-1).astype(jnp.int32)
    pay = lax.all_gather(prep(tokens, out_grad, expert_ids.T, gates.T), "expert")
    x_rows, s_rows, oh = route(q.reshape(1).astype(jnp.int32), pay)
    *blocks_a, d_a = grads(0, where_a, x_rows, s_rows, w_gate_up, w_down)
    *blocks_b, d_b = grads(1, where_b, x_rows, s_rows, w_gate_up, w_down)
    partial = back(d_a, d_b, w_gate_up, oh)
    in_grad = lax.psum_scatter(partial, "expert", scatter_dimension=0, tiled=True)
    a = stage_two(1, *stage_one(0, *blocks_a))
    b = stage_two(0, *stage_one(1, *blocks_b))
    gu, dn = last(*a, *b)
    return in_grad, gu.reshape(GU_ROWS, EXP, 2 * FF), dn.reshape(DN_ROWS, EXP, D)


def solution(mesh):
    spec = P(("dp", "expert"), None)
    return jax.shard_map(
        per_device,
        mesh=mesh,
        in_specs=(spec, spec, spec, spec, P("expert", None, None), P("expert", None, None)),
        out_specs=(spec, P("dp", "expert", None), P("dp", "expert", None)),
        check_vma=False,
    )
```

time: 416 us -> 199 us (0.48)
  waiting for transfers between devices: 256 us -> 102 us
  other arithmetic: 49.2 us -> 0.09 us
  Pallas kernels: 0 us -> 34.1 us
  matrix products: 33.1 us -> 0 us
  local copies, waits for them, and re-layouts: 39.1 us -> 21.7 us
    all_to_all x3 -> x0, waiting for transfers between devices: 194 us -> none  [the longest x1 69.2 us: per_device(): lax.all_to_all(route_grad, 'expert', split_axis=0, concat_axis=0, tiled=T...]
    all_gather x0 -> x1, waiting for transfers between devices: none -> 63.6 us  [per_device(): lax.all_gather(prep(tokens, out_grad, expert_ids.T, gates.T), 'expert')]
    unnamed x2, waiting for transfers between devices: 62.5 us -> 0.03 us
    ppermute x0 -> x16, waiting for transfers between devices: none -> 37.9 us  [move(): return lax.ppermute(block, 'dp', along(axis, step))]
    pallas_call x0 -> x12, Pallas kernels: none -> 34.1 us  [the longest x2 17.2 us: grads(): pl.pallas_call(grads_kernel, out_shape=tuple((shape(n) for n in counts))...]
    dot_general x5 -> x0, matrix products: 33.1 us -> none  [the longest x1 8.47 us: recompute(): jnp.einsum('sjcd,jdf->sjcf', x_recv, w_gate_up, preferred_element_type=jn...]
    another operation x3 -> x0, other arithmetic: 31.3 us -> none
    ppermute x0 -> x16, starting transfers between devices: none -> 23.1 us  [move(): return lax.ppermute(block, 'dp', along(axis, step))]
  transfers between devices with their start and end apart: 4 -> 18, of which waited for: 4 -> 5; matrix products, arithmetic and copies ran while one was open for 9% -> 1% of each run, Pallas kernels for 0% -> 3%
where the time goes in v1:
time: 199 us; the launch traced here: 195 us
  waiting for transfers between devices  102 us (51%)
  Pallas kernels  34.1 us (17%)
  starting transfers between devices  23.1 us (12%)
  local copies, waits for them, and re-layouts  21.7 us (11%)
  between operations  14.3 us (7%)
    all_gather x1, waiting for transfers between devices, per_device(): lax.all_gather(prep(tokens, out_grad, expert_ids.T, gates.T), 'expert')  63.6 us
    ppermute x16, waiting for transfers between devices, move(): return lax.ppermute(block, 'dp', along(axis, step))  37.9 us
    ppermute x16, starting transfers between devices, move(): return lax.ppermute(block, 'dp', along(axis, step))  23.1 us
    unnamed x48, local copies, waits for them, and re-layouts  19.3 us
    pallas_call x2, Pallas kernels, grads(): pl.pallas_call(grads_kernel, out_shape=tuple((shape(n) for n in counts))...  17.2 us
    pallas_call x1, Pallas kernels, route(): pl.pallas_call(route_kernel, out_shape=(rows, rows, jax.ShapeDtypeStruct(...  4.65 us
    pallas_call x1, Pallas kernels, back(): pl.pallas_call(back_kernel, out_shape=jax.ShapeDtypeStruct((OWN * TOK, D)...  4.6 us
    pallas_call x2, Pallas kernels, add3(): pl.pallas_call(add3_kernel, out_shape=(out, out), cost_estimate=pl.CostEs...  4.09 us
  transfers between devices with their start and end apart: 18, of which 5 were waited for; matrix products, arithmetic and copies ran while one was open for 1% of the time, Pallas kernels for 3%

profile of v1, /device:TPU:1, one launch (start us, length us, event | category | flops | bytes accessed | tf_op | source)
XLA Modules:
  0.0 194.8 jit_solution(2244611423053598755)
XLA Ops:
  7.2 0.0 all-gather.3.cloned.1.call-start
  7.2 1.9 shard_map.85
  9.1 0.0 all-gather.3.cloned.1.call-update
  9.1 0.0 reduce-scatter.2.cloned.1.call-start
  9.2 0.1 broadcast_add_fusion
  9.3 0.1 add.109.where_ref
  9.4 0.1 add.105.where_ref
  9.4 63.6 %all-gather.3.cloned.1.call-done = bf16[2048,2176]{1,0:T(8,128)(2,1)} async-done(((bf16[128,2176]{1,0:T(8,128)(2,1)}), bf16[2048,2176]{1,0:T(8,128)(2,1)}) %all-gather.3.cloned.1.call-update) | async-done | bytes 8912912 | tf_op jit(solution)/shard_map/all_gather | solution.py:344
  73.0 3.5 %copy-done.3 = bf16[2048,2176]{1,0:T(8,128)(2,1)S(1)} copy-done((bf16[2048,2176]{1,0:T(8,128)(2,1)S(1)}, bf16[2048,2176]{1,0:T(8,128)(2,1)}, u32[]{:S(2)}) %copy-start.3) | copy-done | bytes 8912920
  76.6 4.7 %shard_map.86 = (bf16[4,384,1024]{2,1,0:T(8,128)(2,1)S(1)}, bf16[4,384,1024]{2,1,0:T(8,128)(2,1)S(1)}, bf16[8,192,256]{2,1,0:T(8,128)(2,1)S(1)}) custom-call(s32[1]{0:T(128)} %bitcast.q_ref, bf16[16,128,2176]{2,1,0:T(8,128)(2,1)S(1)} %bitcast.6), custom_call_target="tpu_custom_call" | custom-call | flops 1610612736 | bytes 15728640 | tf_op jit(solution)/shard_map/pallas_call | solution.py:107
  81.2 1.6 copy-done.1
  82.9 1.7 copy-done.2
  84.5 8.7 %shard_map.88 = (bf16[4,144,1024]{2,1,0:T(8,128)(2,1)S(1)}, bf16[4,144,1024]{2,1,0:T(8,128)(2,1)S(1)}, bf16[4,144,1024]{2,1,0:T(8,128)(2,1)S(1)}, bf16[2,144,102...) custom-call(s32[16]{0:T(128)S(1)} %add.109.where_ref, ...), custom_call_target="tpu_custom_call" | custom-call | flops 3623878656 | bytes 12582912 | tf_op jit(solution)/shard_map/pallas_call | solution.py:171
  93.3 1.0 copy-done.6
  94.3 1.1 copy-done.8
  95.4 0.8 copy-done.16
  96.2 0.8 copy-done.17
  97.0 8.5 %shard_map.87 = (bf16[4,144,1024]{2,1,0:T(8,128)(2,1)S(1)}, bf16[4,144,1024]{2,1,0:T(8,128)(2,1)S(1)}, bf16[4,144,1024]{2,1,0:T(8,128)(2,1)S(1)}, bf16[2,144,102...) custom-call(s32[16]{0:T(128)S(1)} %add.105.where_ref, ...), custom_call_target="tpu_custom_call" | custom-call | flops 3623878656 | bytes 12582912 | tf_op jit(solution)/shard_map/pallas_call | solution.py:171
  105.6 1.0 copy-done.4
  106.6 0.8 copy-done.14
  107.4 0.8 copy-done.15
  108.3 4.6 %shard_map.89 = bf16[2048,1024]{1,0:T(8,128)(2,1)S(1)} custom-call(bf16[2,384,768]{2,1,0:T(8,128)(2,1)S(1)} %get-tuple-element.40.da_ref, bf16[2,384,768]{2,1,0:T(8,128)(2,1)S(1)} %get-tuple-element.41.db_ref, bf16[4,1024,768]{2,1,0:T(8,128)(2,1)S(1)} %bitcast.5, bf16[8,192,256]{2,1,0:T(8,128)(2,1)S(1)} %get-tuple-element.42.oh_ref), custom_call_target="tpu_custom_call" | custom-call | flops 3221225472 | bytes 16777216 | tf_op jit(solution)/shard_map/pallas_call | solution.py:210
  112.9 2.0 %copy-done = bf16[2048,1024]{1,0:T(8,128)(2,1)} copy-done((bf16[2048,1024]{1,0:T(8,128)(2,1)}, bf16[2048,1024]{1,0:T(8,128)(2,1)S(1)}, u32[]{:S(2)}) %copy-start) | copy-done | bytes 4194328
  114.9 0.0 reduce-scatter.2.cloned.1.call-update
  114.9 1.3 collective-permute-start.8
  116.2 1.5 collective-permute-start.9
  117.6 1.2 collective-permute-start
  118.8 1.5 collective-permute-start.1
  120.3 10.8 %collective-permute-done.8.ra = bf16[2,144,1024]{2,1,0:T(8,128)(2,1)S(1)} collective-permute-done((bf16[2,144,1024]{2,1,0:T(8,128)(2,1)}, bf16[2,144,1024]{2,1,0:T(8,128)(2,1)S(1)}, u32[]{:S(2)}, u32[]{:S(2)}) %collective-permute-start.8) | collective-permute-done | bytes 589856 | tf_op jit(solution)/shard_map/ppermute | solution.py:321
  131.2 0.0 collective-permute-done.9.rb
  131.2 1.3 copy-done.7
  132.5 1.3 copy-done.9
  133.7 0.3 shard_map.93
  134.1 1.0 collective-permute-start.10
  135.0 1.8 collective-permute-start.11
  136.8 0.0 collective-permute-done.ra
  136.8 0.0 collective-permute-done.1.rb
  136.8 0.3 shard_map.90
  137.1 1.3 collective-permute-start.2
  138.4 1.5 collective-permute-start.3
  139.9 22.0 %collective-permute-done.10.r1 = bf16[4,144,1024]{2,1,0:T(8,128)(2,1)S(1)} collective-permute-done((bf16[4,144,1024]{2,1,0:T(8,128)(2,1)S(1)}, bf16[4,144,1024]{2,1,0:T(8,128)(2,1)S(1)}, u32[]{:S(2)}, u32[]{:S(2)}) %collective-permute-start.10) | collective-permute-done | bytes 1179680 | tf_op jit(solution)/shard_map/ppermute | solution.py:321
  161.9 0.4 shard_map.94
  162.3 1.4 collective-permute-start.12
  163.7 0.8 collective-permute-done.2.r1
  164.5 0.4 shard_map.91
  164.9 0.0 copy-start.10
  164.9 0.0 copy-start.11
  164.9 0.1 collective-permute-start.4
  165.0 2.5 %collective-permute-start.13 = (bf16[64,1024]{1,0:T(8,128)(2,1)S(1)}, bf16[64,1024]{1,0:T(8,128)(2,1)S(1)}, u32[]{:S(2)}, u32[]{:S(2)}) collective-permute-start(bf16[64,1024]{1,0:T(8,128)(2,1)S(1)} %get-tuple-element.68), channel_id=1, source_target_pairs={{0,192},{16,208},{32,224},{48,240},{64,0},{80,16},{96,32},{112,48}... | collective-permute-start | bytes 393224 | tf_op jit(solution)/shard_map/ppermute | solution.py:321
  167.5 2.6 %collective-permute-start.5 = (bf16[64,1024]{1,0:T(8,128)(2,1)S(1)}, bf16[64,1024]{1,0:T(8,128)(2,1)S(1)}, u32[]{:S(2)}, u32[]{:S(2)}) collective-permute-start(bf16[64,1024]{1,0:T(8,128)(2,1)S(1)} %get-tuple-element.54), channel_id=1, source_target_pairs={{0,48},{16,0},{32,16},{48,32},{64,112},{80,64},{96,80},{112,96},{1... | collective-permute-start | bytes 393224 | tf_op jit(solution)/shard_map/ppermute | solution.py:321
  170.1 0.6 copy-done.21
  170.7 0.1 copy-done.19
  170.8 2.1 %shard_map.95 = (bf16[144,1024]{1,0:T(8,128)(2,1)}, bf16[144,1024]{1,0:T(8,128)(2,1)}) custom-call(bf16[144,1024]{1,0:T(8,128)(2,1)} %copy-done.12, bf16[80,1024]{1,0:T(8,128)(2,1)} %copy-done.19, bf16[144,1024]{1,0:T(8,128)(2,1)} %copy-done.13, bf16[64,1024]{1,0:T(8,128)(2,1)} %copy-done.21), custom_call_target="tpu_custom_call" | custom-call | bytes 1048576 | tf_op jit(solution)/shard_map/pallas_call | solution.py:281
  172.9 0.1 collective-permute-start.14
  173.0 2.8 %collective-permute-start.15 = (bf16[144,1024]{1,0:T(8,128)(2,1)}, bf16[144,1024]{1,0:T(8,128)(2,1)S(1)}, u32[]{:S(2)}, u32[]{:S(2)}) collective-permute-start(bf16[144,1024]{1,0:T(8,128)(2,1)} %get-tuple-element.70), channel_id=1, source_target_pairs={{0,192},{16,208},{32,224},{48,240},{64,0},{80,16},{96,32},{112,48}... | collective-permute-start | bytes 884744 | tf_op jit(solution)/shard_map/ppermute | solution.py:321
  175.8 0.6 copy-done.20
  176.4 0.1 copy-done.18
  176.5 2.0 %shard_map.92 = (bf16[144,1024]{1,0:T(8,128)(2,1)}, bf16[144,1024]{1,0:T(8,128)(2,1)}) custom-call(bf16[144,1024]{1,0:T(8,128)(2,1)} %copy-done.10, bf16[80,1024]{1,0:T(8,128)(2,1)} %copy-done.18, bf16[144,1024]{1,0:T(8,128)(2,1)} %copy-done.11, bf16[64,1024]{1,0:T(8,128)(2,1)} %copy-done.20), custom_call_target="tpu_custom_call" | custom-call | bytes 1048576 | tf_op jit(solution)/shard_map/pallas_call | solution.py:281
  178.5 0.2 collective-permute-start.6
  178.7 2.5 %collective-permute-start.7 = (bf16[144,1024]{1,0:T(8,128)(2,1)}, bf16[144,1024]{1,0:T(8,128)(2,1)S(1)}, u32[]{:S(2)}, u32[]{:S(2)}) collective-permute-start(bf16[144,1024]{1,0:T(8,128)(2,1)} %get-tuple-element.56), channel_id=1, source_target_pairs={{0,48},{16,0},{32,16},{48,32},{64,112},{80,64},{96,80},{112,96},{1... | collective-permute-start | bytes 884744 | tf_op jit(solution)/shard_map/ppermute | solution.py:321
  181.2 4.3 %collective-permute-done.6.a1 = bf16[144,1024]{1,0:T(8,128)(2,1)S(1)} collective-permute-done((bf16[144,1024]{1,0:T(8,128)(2,1)}, bf16[144,1024]{1,0:T(8,128)(2,1)S(1)}, u32[]{:S(2)}, u32[]{:S(2)}) %collective-permute-start.6) | collective-permute-done | bytes 294944 | tf_op jit(solution)/shard_map/ppermute | solution.py:321
  185.5 0.2 shard_map.96
  185.7 1.3 reshape.88
  187.0 1.0 reshape.89
  (41 shorter events, 0.1 us)
Async XLA Ops:
  7.2 65.9 %all-gather.3.cloned.1.call-start = ((), (), s32[]{:S(2)}) async-start(), calls=%async_computation.2 | async-start | bytes 9469952 | tf_op jit(solution)/shard_map/all_gather | solution.py:344
  9.1 178.9 %reduce-scatter.2.cloned.1.call-start = ((), (), s32[]{:S(2)}) async-start(), calls=%async_computation.1 | async-start | bytes 4456448 | tf_op jit(solution)/shard_map/reduce_scatter | solution.py:349
  73.0 3.5 %copy-start.3 = (bf16[2048,2176]{1,0:T(8,128)(2,1)S(1)}, bf16[2048,2176]{1,0:T(8,128)(2,1)}, u32[]{:S(2)}) copy-start(bf16[2048,2176]{1,0:T(8,128)(2,1)} %all-gather.3.cloned.1.call-done) | copy-start | bytes 26738692
  81.2 1.6 copy-start.1
  82.9 1.7 copy-start.2
  84.5 23.7 %slice-start = ((s8[6291456]{0:T(1024)(128)(4,1)}), s8[4194304]{0:T(1024)(128)(4,1)S(1)}, s32[]{:S(2)}) async-start(s8[6291456]{0:T(1024)(128)(4,1)} %bitcast.4), calls=%async_computation.3 | async-start | bytes 8388608
  93.2 1.0 copy-start.6
  94.3 1.1 copy-start.8
  95.4 0.8 copy-start.16
  96.2 0.8 copy-start.17
  97.0 11.2 %slice-start.1 = ((s8[6291456]{0:T(1024)(128)(4,1)}), s8[2097152]{0:T(1024)(128)(4,1)S(1)}, s32[]{:S(2)}) async-start(s8[6291456]{0:T(1024)(128)(4,1)} %bitcast.4), calls=%async_computation.4 | async-start | bytes 4194304
  105.6 1.0 copy-start.4
  106.6 0.8 copy-start.14
  107.4 0.8 copy-start.15
  112.9 2.0 %copy-start = (bf16[2048,1024]{1,0:T(8,128)(2,1)}, bf16[2048,1024]{1,0:T(8,128)(2,1)S(1)}, u32[]{:S(2)}) copy-start(bf16[2048,1024]{1,0:T(8,128)(2,1)S(1)} %shard_map.89) | copy-start | bytes 12582916
  114.9 16.3 %collective-permute-start.8 = (bf16[2,144,1024]{2,1,0:T(8,128)(2,1)}, bf16[2,144,1024]{2,1,0:T(8,128)(2,1)S(1)}, u32[]{:S(2)}, u32[]{:S(2)}) collective-permute-start(bf16[2,144,1024]{2,1,0:T(8,128)(2,1)} %copy-done.17), channel_id=1, source_target_pairs={{0,16},{16,32},{32,48},{48,0},{64,80},{80,96},{96,112},{112,64},{1... | collective-permute-start | bytes 1769480 | tf_op jit(solution)/shard_map/ppermute | solution.py:321
  116.2 15.0 %collective-permute-start.9 = (bf16[2,144,1024]{2,1,0:T(8,128)(2,1)}, bf16[2,144,1024]{2,1,0:T(8,128)(2,1)S(1)}, u32[]{:S(2)}, u32[]{:S(2)}) collective-permute-start(bf16[2,144,1024]{2,1,0:T(8,128)(2,1)} %copy-done.16), channel_id=1, source_target_pairs={{0,48},{16,0},{32,16},{48,32},{64,112},{80,64},{96,80},{112,96},{1... | collective-permute-start | bytes 1769480 | tf_op jit(solution)/shard_map/ppermute | solution.py:321
  117.6 19.2 %collective-permute-start = (bf16[2,144,1024]{2,1,0:T(8,128)(2,1)}, bf16[2,144,1024]{2,1,0:T(8,128)(2,1)S(1)}, u32[]{:S(2)}, u32[]{:S(2)}) collective-permute-start(bf16[2,144,1024]{2,1,0:T(8,128)(2,1)} %copy-done.15), channel_id=1, source_target_pairs={{0,64},{16,80},{32,96},{48,112},{64,128},{80,144},{96,160},{112,17... | collective-permute-start | bytes 1769480 | tf_op jit(solution)/shard_map/ppermute | solution.py:321
  118.8 18.0 %collective-permute-start.1 = (bf16[2,144,1024]{2,1,0:T(8,128)(2,1)}, bf16[2,144,1024]{2,1,0:T(8,128)(2,1)S(1)}, u32[]{:S(2)}, u32[]{:S(2)}) collective-permute-start(bf16[2,144,1024]{2,1,0:T(8,128)(2,1)} %copy-done.14), channel_id=1, source_target_pairs={{0,192},{16,208},{32,224},{48,240},{64,0},{80,16},{96,32},{112,48}... | collective-permute-start | bytes 1769480 | tf_op jit(solution)/shard_map/ppermute | solution.py:321
  131.2 1.3 copy-start.7
  132.5 1.3 copy-start.9
  133.7 3.1 %copy-start.5 = (bf16[4,144,1024]{2,1,0:T(8,128)(2,1)S(1)}, bf16[4,144,1024]{2,1,0:T(8,128)(2,1)}, u32[]{:S(2)}) copy-start(bf16[4,144,1024]{2,1,0:T(8,128)(2,1)} %copy-done.4) | copy-start | bytes 3538948
  134.1 27.8 %collective-permute-start.10 = (bf16[4,144,1024]{2,1,0:T(8,128)(2,1)S(1)}, bf16[4,144,1024]{2,1,0:T(8,128)(2,1)S(1)}, u32[]{:S(2)}, u32[]{:S(2)}) collective-permute-start(bf16[4,144,1024]{2,1,0:T(8,128)(2,1)S(1)} %get-tuple-element.62), channel_id=1, source_target_pairs={{0,16},{16,32},{32,48},{48,0},{64,80},{80,96},{96,112},{112,64},{1... | collective-permute-start | bytes 3538952 | tf_op jit(solution)/shard_map/ppermute | solution.py:321
  135.0 26.8 %collective-permute-start.11 = (bf16[4,144,1024]{2,1,0:T(8,128)(2,1)S(1)}, bf16[4,144,1024]{2,1,0:T(8,128)(2,1)S(1)}, u32[]{:S(2)}, u32[]{:S(2)}) collective-permute-start(bf16[4,144,1024]{2,1,0:T(8,128)(2,1)S(1)} %get-tuple-element.63), channel_id=1, source_target_pairs={{0,48},{16,0},{32,16},{48,32},{64,112},{80,64},{96,80},{112,96},{1... | collective-permute-start | bytes 3538952 | tf_op jit(solution)/shard_map/ppermute | solution.py:321
  137.1 27.3 %collective-permute-start.2 = (bf16[4,144,1024]{2,1,0:T(8,128)(2,1)S(1)}, bf16[4,144,1024]{2,1,0:T(8,128)(2,1)S(1)}, u32[]{:S(2)}, u32[]{:S(2)}) collective-permute-start(bf16[4,144,1024]{2,1,0:T(8,128)(2,1)S(1)} %get-tuple-element.48), channel_id=1, source_target_pairs={{0,64},{16,80},{32,96},{48,112},{64,128},{80,144},{96,160},{112,17... | collective-permute-start | bytes 3538952 | tf_op jit(solution)/shard_map/ppermute | solution.py:321
  138.4 26.1 %collective-permute-start.3 = (bf16[4,144,1024]{2,1,0:T(8,128)(2,1)S(1)}, bf16[4,144,1024]{2,1,0:T(8,128)(2,1)S(1)}, u32[]{:S(2)}, u32[]{:S(2)}) collective-permute-start(bf16[4,144,1024]{2,1,0:T(8,128)(2,1)S(1)} %get-tuple-element.49), channel_id=1, source_target_pairs={{0,192},{16,208},{32,224},{48,240},{64,0},{80,16},{96,32},{112,48}... | collective-permute-start | bytes 3538952 | tf_op jit(solution)/shard_map/ppermute | solution.py:321
  162.3 2.6 %copy-start.12 = (bf16[144,1024]{1,0:T(8,128)(2,1)}, bf16[144,1024]{1,0:T(8,128)(2,1)S(1)}, u32[]{:S(2)}) copy-start(bf16[144,1024]{1,0:T(8,128)(2,1)S(1)} %get-tuple-element.65.f1) | copy-start | bytes 884740
  162.3 2.6 %copy-start.13 = (bf16[144,1024]{1,0:T(8,128)(2,1)}, bf16[144,1024]{1,0:T(8,128)(2,1)S(1)}, u32[]{:S(2)}) copy-start(bf16[144,1024]{1,0:T(8,128)(2,1)S(1)} %get-tuple-element.67.f3) | copy-start | bytes 884740
  162.3 7.8 %collective-permute-start.12 = (bf16[80,1024]{1,0:T(8,128)(2,1)S(1)}, bf16[80,1024]{1,0:T(8,128)(2,1)S(1)}, u32[]{:S(2)}, u32[]{:S(2)}) collective-permute-start(bf16[80,1024]{1,0:T(8,128)(2,1)S(1)} %get-tuple-element.66), channel_id=1, source_target_pairs={{0,64},{16,80},{32,96},{48,112},{64,128},{80,144},{96,160},{112,17... | collective-permute-start | bytes 491528 | tf_op jit(solution)/shard_map/ppermute | solution.py:321
  164.9 8.0 %copy-start.10 = (bf16[144,1024]{1,0:T(8,128)(2,1)}, bf16[144,1024]{1,0:T(8,128)(2,1)S(1)}, u32[]{:S(2)}) copy-start(bf16[144,1024]{1,0:T(8,128)(2,1)S(1)} %get-tuple-element.51.f1) | copy-start | bytes 884740
  164.9 8.0 %copy-start.11 = (bf16[144,1024]{1,0:T(8,128)(2,1)}, bf16[144,1024]{1,0:T(8,128)(2,1)S(1)}, u32[]{:S(2)}) copy-start(bf16[144,1024]{1,0:T(8,128)(2,1)S(1)} %get-tuple-element.53.f3) | copy-start | bytes 884740
  164.9 10.9 %collective-permute-start.4 = (bf16[80,1024]{1,0:T(8,128)(2,1)S(1)}, bf16[80,1024]{1,0:T(8,128)(2,1)S(1)}, u32[]{:S(2)}, u32[]{:S(2)}) collective-permute-start(bf16[80,1024]{1,0:T(8,128)(2,1)S(1)} %get-tuple-element.52), channel_id=1, source_target_pairs={{0,16},{16,32},{32,48},{48,0},{64,80},{80,96},{96,112},{112,64},{1... | collective-permute-start | bytes 491528 | tf_op jit(solution)/shard_map/ppermute | solution.py:321
  165.0 5.1 %collective-permute-start.13 = (bf16[64,1024]{1,0:T(8,128)(2,1)S(1)}, bf16[64,1024]{1,0:T(8,128)(2,1)S(1)}, u32[]{:S(2)}, u32[]{:S(2)}) collective-permute-start(bf16[64,1024]{1,0:T(8,128)(2,1)S(1)} %get-tuple-element.68), channel_id=1, source_target_pairs={{0,192},{16,208},{32,224},{48,240},{64,0},{80,16},{96,32},{112,48}... | collective-permute-start | bytes 393224 | tf_op jit(solution)/shard_map/ppermute | solution.py:321
  167.5 8.3 %collective-permute-start.5 = (bf16[64,1024]{1,0:T(8,128)(2,1)S(1)}, bf16[64,1024]{1,0:T(8,128)(2,1)S(1)}, u32[]{:S(2)}, u32[]{:S(2)}) collective-permute-start(bf16[64,1024]{1,0:T(8,128)(2,1)S(1)} %get-tuple-element.54), channel_id=1, source_target_pairs={{0,48},{16,0},{32,16},{48,32},{64,112},{80,64},{96,80},{112,96},{1... | collective-permute-start | bytes 393224 | tf_op jit(solution)/shard_map/ppermute | solution.py:321
  170.1 0.6 copy-start.21
  170.1 0.7 copy-start.19
  172.9 8.4 %collective-permute-start.14 = (bf16[144,1024]{1,0:T(8,128)(2,1)}, bf16[144,1024]{1,0:T(8,128)(2,1)S(1)}, u32[]{:S(2)}, u32[]{:S(2)}) collective-permute-start(bf16[144,1024]{1,0:T(8,128)(2,1)} %get-tuple-element.69), channel_id=1, source_target_pairs={{0,64},{16,80},{32,96},{48,112},{64,128},{80,144},{96,160},{112,17... | collective-permute-start | bytes 884744 | tf_op jit(solution)/shard_map/ppermute | solution.py:321
  173.0 8.3 %collective-permute-start.15 = (bf16[144,1024]{1,0:T(8,128)(2,1)}, bf16[144,1024]{1,0:T(8,128)(2,1)S(1)}, u32[]{:S(2)}, u32[]{:S(2)}) collective-permute-start(bf16[144,1024]{1,0:T(8,128)(2,1)} %get-tuple-element.70), channel_id=1, source_target_pairs={{0,192},{16,208},{32,224},{48,240},{64,0},{80,16},{96,32},{112,48}... | collective-permute-start | bytes 884744 | tf_op jit(solution)/shard_map/ppermute | solution.py:321
  175.8 0.6 copy-start.20
  175.8 0.7 copy-start.18
  178.5 7.0 %collective-permute-start.6 = (bf16[144,1024]{1,0:T(8,128)(2,1)}, bf16[144,1024]{1,0:T(8,128)(2,1)S(1)}, u32[]{:S(2)}, u32[]{:S(2)}) collective-permute-start(bf16[144,1024]{1,0:T(8,128)(2,1)} %get-tuple-element.55), channel_id=1, source_target_pairs={{0,16},{16,32},{32,48},{48,0},{64,80},{80,96},{96,112},{112,64},{1... | collective-permute-start | bytes 884744 | tf_op jit(solution)/shard_map/ppermute | solution.py:321
  178.7 6.8 %collective-permute-start.7 = (bf16[144,1024]{1,0:T(8,128)(2,1)}, bf16[144,1024]{1,0:T(8,128)(2,1)S(1)}, u32[]{:S(2)}, u32[]{:S(2)}) collective-permute-start(bf16[144,1024]{1,0:T(8,128)(2,1)} %get-tuple-element.56), channel_id=1, source_target_pairs={{0,48},{16,0},{32,16},{48,32},{64,112},{80,64},{96,80},{112,96},{1... | collective-permute-start | bytes 884744 | tf_op jit(solution)/shard_map/ppermute | solution.py:321
Sparse Core Ops, SparseCore 0:
  10.4 62.5 all-gather.2
  115.0 58.8 reduce-scatter.1
